TPU v7x, 32 devices: a whole 2x2x4 slice. The times are simulated.
32 devices in a mesh: dp: 4 (over z), ctx: 4 (over y, core), tensor: 2 (over x).
Axes of the slice: x: 2, y: 2, z: 4, core: 2. Of those that a mesh axis runs over, the one named last changes fastest.
Arguments:
- inputs: bfloat16 [2048, 8192], P(('dp', 'ctx')), may hold values from -6 to 6
- value_weight: bfloat16 [8192, 256], P(None, 'tensor'), may hold values from -0.0625 to 0.0625
- queries: bfloat16 [2048, 2048], P(('dp', 'ctx'), 'tensor'), may hold values from -8 to 8
- keys: bfloat16 [2048, 256], P(('dp', 'ctx'), 'tensor'), may hold values from -8 to 8
- out_grad: bfloat16 [2048, 2048], P(('dp', 'ctx'), 'tensor'), may hold values from -6 to 6
- doc_tiles: int32 [8, 3], P('dp'), may hold values from 1 to 12, 16 in all within a row
- route: int32 [4, 4, 4], P(None, 'ctx'), may hold values from 0 to 3, as said below
Outputs:
- query_grad: bfloat16 [2048, 2048], P(('dp', 'ctx'), 'tensor')
- key_grad: bfloat16 [2048, 256], P(('dp', 'ctx'), 'tensor')
- weight_grad: float32 [8192, 256], P(('dp', 'ctx'), 'tensor')
Inputs may be any that keep to these rules, and one draw needn't show every extreme that they name: `doc_tiles`: each row sums to 16 and its largest entry is exactly 12. `route`: the 4 groups of one device go to 4 different data ranks, and at each context index every data rank takes exactly 4 groups.
All inputs are finite; a program needn't handle non-finite values.
Results may differ from a plain program's by a relative error of at most 0.012.
Values may be sent and summed in bfloat16 or wider, within the bound.
A program may use at most 64 MiB of HBM per device.

v0:
```python
import math

import jax
import jax.numpy as jnp
from jax import lax
from jax.sharding import PartitionSpec as P

TILE = 16


def doc_numbers(positions, lengths):
    doc_ends = jnp.cumsum(lengths) * TILE
    return jnp.sum((positions[:, None] >= doc_ends[None, :]).astype(jnp.int32), axis=1)


def local(inputs, value_weight, queries, keys, out_grad, doc_tiles, route):
    tok_rows = inputs.shape[0]
    head_size = keys.shape[1]
    head_count = queries.shape[1] // head_size
    data_ranks = lax.axis_size("dp")
    context_ranks = lax.axis_size("ctx")
    groups = route.shape[2]
    group_rows = tok_rows // groups
    own_rank = lax.axis_index("dp")
    values = jnp.dot(inputs, value_weight, preferred_element_type=jnp.float32).astype(jnp.bfloat16)
    routing = route[:, 0, :]
    rank_ids = jnp.arange(data_ranks, dtype=jnp.int32)
    outgoing = (routing[own_rank][None, :] == rank_ids[:, None]).astype(jnp.bfloat16)
    arrivals = jnp.sum((routing == own_rank).astype(jnp.int32), axis=1)
    before = jnp.cumsum(arrivals) - arrivals
    slot_ids = jnp.arange(groups, dtype=jnp.int32)
    incoming = ((before[None, :] == slot_ids[:, None]) & (arrivals[None, :] > 0)).astype(
        jnp.bfloat16
    )

    def pack_out(rows_block):
        pieces = rows_block.reshape(groups, group_rows, rows_block.shape[1])
        outbound = jnp.einsum("ej,jrc->erc", outgoing, pieces, preferred_element_type=jnp.float32)
        return outbound.astype(jnp.bfloat16).reshape(data_ranks * group_rows, rows_block.shape[1])

    def unpack_in(rows_block):
        pieces = rows_block.reshape(data_ranks, group_rows, rows_block.shape[1])
        selected = jnp.einsum("ks,src->krc", incoming, pieces, preferred_element_type=jnp.float32)
        return selected.astype(jnp.bfloat16).reshape(tok_rows, rows_block.shape[1])

    def pack_back(rows_block):
        pieces = rows_block.reshape(groups, group_rows, rows_block.shape[1])
        outbound = jnp.einsum("ks,krc->src", incoming, pieces, preferred_element_type=jnp.float32)
        return outbound.astype(jnp.bfloat16).reshape(data_ranks * group_rows, rows_block.shape[1])

    def unpack_back(rows_block):
        pieces = rows_block.reshape(data_ranks, group_rows, rows_block.shape[1])
        selected = jnp.einsum("ej,erc->jrc", outgoing, pieces, preferred_element_type=jnp.float32)
        return selected.astype(jnp.bfloat16).reshape(tok_rows, rows_block.shape[1])

    arrived = (
        lax.all_to_all(pack_out(queries), "dp", split_axis=0, concat_axis=0, tiled=True),
        lax.all_to_all(pack_out(keys), "dp", split_axis=0, concat_axis=0, tiled=True),
        lax.all_to_all(pack_out(values), "dp", split_axis=0, concat_axis=0, tiled=True),
    )
    query_rows = unpack_in(arrived[0])
    key_rows = unpack_in(arrived[1])
    value_rows = unpack_in(arrived[2])
    key_all, value_all = (
        lax.all_gather(key_rows, "ctx", axis=0, tiled=True),
        lax.all_gather(value_rows, "ctx", axis=0, tiled=True),
    )
    pack_count = doc_tiles.shape[0]
    seg_rows = tok_rows // pack_count
    pack_len = context_ranks * seg_rows
    key_four = key_all.reshape(context_ranks, pack_count, seg_rows, head_size)
    value_four = value_all.reshape(context_ranks, pack_count, seg_rows, head_size)
    query_pos = lax.axis_index("ctx") * seg_rows + jnp.arange(seg_rows, dtype=jnp.int32)
    key_pos = jnp.arange(pack_len, dtype=jnp.int32)
    query_doc = jax.vmap(lambda lengths: doc_numbers(query_pos, lengths))(doc_tiles)
    key_doc = jax.vmap(lambda lengths: doc_numbers(key_pos, lengths))(doc_tiles)
    allowed = (query_doc[:, :, None] == key_doc[:, None, :]) & (
        key_pos[None, None, :] <= query_pos[None, :, None]
    )
    score_scale = 1.0 / math.sqrt(head_size)
    query_heads = query_rows.reshape(pack_count, seg_rows, head_count, head_size)
    grad_heads = out_grad.reshape(pack_count, seg_rows, head_count, head_size)
    split_shape = (pack_count, head_count, seg_rows, context_ranks, seg_rows)
    flat_shape = (pack_count, head_count, seg_rows, pack_len)
    scores = (
        jnp.einsum(
            "qthd,cqsd->qhtcs", query_heads, key_four, preferred_element_type=jnp.float32
        ).reshape(flat_shape)
        * score_scale
    )
    scores = jnp.where(allowed[:, None], scores, -jnp.inf)
    row_peak = jnp.max(scores, axis=3, keepdims=True)
    weights = jnp.exp(scores - row_peak)
    attention = weights / jnp.sum(weights, axis=3, keepdims=True)
    attention_low = attention.astype(jnp.bfloat16).reshape(split_shape)
    attended = jnp.einsum(
        "qhtcs,cqsd->qthd", attention_low, value_four, preferred_element_type=jnp.float32
    ).astype(jnp.bfloat16)
    row_inner = jnp.sum(grad_heads.astype(jnp.float32) * attended.astype(jnp.float32), axis=3)
    grad_probs = jnp.einsum(
        "qthd,cqsd->qhtcs", grad_heads, value_four, preferred_element_type=jnp.float32
    ).reshape(flat_shape)
    grad_scores = (
        attention * (grad_probs - jnp.transpose(row_inner, (0, 2, 1))[:, :, :, None]) * score_scale
    ).astype(jnp.bfloat16)
    grad_split = grad_scores.reshape(split_shape)
    query_here = jnp.einsum(
        "qhtcs,cqsd->qthd", grad_split, key_four, preferred_element_type=jnp.float32
    ).astype(jnp.bfloat16)
    query_here = query_here.reshape(tok_rows, head_count * head_size)
    key_total = jnp.einsum(
        "qhtcs,qthd->cqsd", grad_split, query_heads, preferred_element_type=jnp.float32
    ).reshape(context_ranks * tok_rows, head_size)
    value_total = jnp.einsum(
        "qhtcs,qthd->cqsd", attention_low, grad_heads, preferred_element_type=jnp.float32
    ).reshape(context_ranks * tok_rows, head_size)
    key_own, value_own = (
        lax.psum_scatter(key_total, "ctx", scatter_dimension=0, tiled=True),
        lax.psum_scatter(value_total, "ctx", scatter_dimension=0, tiled=True),
    )
    returned = (
        lax.all_to_all(pack_back(query_here), "dp", split_axis=0, concat_axis=0, tiled=True),
        lax.all_to_all(
            pack_back(key_own.astype(jnp.bfloat16)), "dp", split_axis=0, concat_axis=0, tiled=True
        ),
        lax.all_to_all(
            pack_back(value_own.astype(jnp.bfloat16)), "dp", split_axis=0, concat_axis=0, tiled=True
        ),
    )
    query_grad = unpack_back(returned[0])
    key_grad = unpack_back(returned[1])
    value_grad = unpack_back(returned[2])
    weight_grad = lax.psum_scatter(
        jnp.einsum("tr,th->rh", inputs, value_grad, preferred_element_type=jnp.float32),
        ("dp", "ctx"),
        scatter_dimension=0,
        tiled=True,
    )
    return (query_grad, key_grad, weight_grad)


def solution(mesh):
    in_specs = (
        P(("dp", "ctx"), None),
        P(None, "tensor"),
        P(("dp", "ctx"), "tensor"),
        P(("dp", "ctx"), "tensor"),
        P(("dp", "ctx"), "tensor"),
        P("dp", None),
        P(None, "ctx", None),
    )
    out_specs = (P(("dp", "ctx"), "tensor"), P(("dp", "ctx"), "tensor"), P(("dp", "ctx"), "tensor"))
    return jax.shard_map(local, mesh=mesh, in_specs=in_specs, out_specs=out_specs, check_vma=False)
```

profile of v0, /device:TPU:0, one launch (start us, length us, event | category | flops | bytes accessed | tf_op | source)
XLA Modules:
  0.0 189.0 jit_solution(18162925487847567890)
XLA Ops:
  7.2 0.8 dynamic-slice_bitcast_fusion
  8.0 0.8 copy-done
  8.8 2.3 %convolution_convert_fusion.10 = bf16[128,128]{1,0:T(8,128)(2,1)S(1)} fusion(bf16[128,8192]{1,0:T(8,128)(2,1)S(1)} %copy-done, bf16[8192,128]{1,0:T(8,128)(2,1)} %param.8), kind=kOutput, calls=%fused_computation.30 | convolution fusion | flops 268451840 | bytes 4227072 | tf_op jit(solution)/shard_map/dot_general | solution.py:25
  11.2 0.3 convolution_convert_fusion.9
  11.4 0.6 copy.97
  12.1 6.3 %all-to-all-start.2 = ((bf16[4,32,128]{2,1,0:T(8,128)(2,1)}), bf16[4,32,128]{2,1,0:T(8,128)(2,1)S(1)}, u32[]{:S(2)}, u32[]{:S(2)}) async-start(bf16[4,32,128]{2,1,0:T(8,128)(2,1)} %copy.97), calls=%async_computation.2 | async-start | bytes 65536 | tf_op jit(solution)/shard_map/all_to_all | solution.py:59
  18.4 0.2 fusion.37
  18.6 0.2 reduce-window.8
  18.8 0.2 reduce_window_sum.19
  19.3 0.1 broadcast_compare_fusion
  19.4 0.3 convolution_convert_fusion.12
  19.8 0.7 copy-done.2
  20.5 0.7 bitcast_bitcast_fusion.1
  21.2 0.4 convolution_convert_fusion.3
  21.6 0.1 compare_and_fusion
  21.8 0.6 copy.81
  22.4 1.6 all-to-all-done.2
  24.0 3.5 %all-to-all-start = ((bf16[4,32,128]{2,1,0:T(8,128)(2,1)}), bf16[4,32,128]{2,1,0:T(8,128)(2,1)S(1)}, u32[]{:S(2)}, u32[]{:S(2)}) async-start(bf16[4,32,128]{2,1,0:T(8,128)(2,1)} %copy.81), calls=%async_computation | async-start | bytes 65536 | tf_op jit(solution)/shard_map/all_to_all | solution.py:58
  27.6 0.8 copy.89
  28.4 4.8 %all-to-all-done = bf16[4,32,128]{2,1,0:T(8,128)(2,1)S(1)} async-done(((bf16[4,32,128]{2,1,0:T(8,128)(2,1)}), bf16[4,32,128]{2,1,0:T(8,128)(2,1)S(1)}, u32[]{:S(2)}, u32[]{:S(2)}) %all-to-all-start) | async-done | bytes 32800 | tf_op jit(solution)/shard_map/all_to_all | solution.py:58
  33.2 3.4 %all-to-all-start.1 = ((bf16[4,32,1024]{2,1,0:T(8,128)(2,1)}), bf16[4,32,1024]{2,1,0:T(8,128)(2,1)S(1)}, u32[]{:S(2)}, u32[]{:S(2)}) async-start(bf16[4,32,1024]{2,1,0:T(8,128)(2,1)} %copy.89), calls=%async_computation.1 | async-start | bytes 524288 | tf_op jit(solution)/shard_map/all_to_all | solution.py:57
  36.6 0.2 convolution_convert_fusion.8
  36.9 0.2 convolution_convert_fusion.11
  37.1 5.4 %all_gather.6 = bf16[512,128]{1,0:T(8,128)(2,1)S(1)} all-gather(bf16[128,128]{1,0:T(8,128)(2,1)S(1)} %bitcast.147), channel_id=1, replica_groups=mesh['dp'=4,'ctx'=4,'tensor'=2] {'ctx'}, dimensions={0}, use_global_device_ids=true | all-gather | bytes 163840 | tf_op jit(solution)/shard_map/all_gather | solution.py:65
  42.5 5.9 %all_gather.7 = bf16[512,128]{1,0:T(8,128)(2,1)} all-gather(bf16[128,128]{1,0:T(8,128)(2,1)S(1)} %bitcast.146), channel_id=1, replica_groups=mesh['dp'=4,'ctx'=4,'tensor'=2] {'ctx'}, dimensions={0}, use_global_device_ids=true | all-gather | bytes 163840 | tf_op jit(solution)/shard_map/all_gather | solution.py:66
  48.4 0.3 convolution_convert_fusion.2
  48.9 0.5 fusion.47
  49.5 0.4 fusion.4
  49.8 0.4 fusion.14
  50.2 0.6 copy-done.1
  50.8 0.2 copy-done.4
  51.0 0.4 convolution_bitcast_fusion.3
  51.3 0.7 copy.120
  52.1 1.6 fusion.10
  53.7 2.5 %fusion.2 = bf16[2,8,64,4,64]{2,4,1,3,0:T(8,128)(2,1)S(1)} fusion(f32[2,8,64]{2,1,0:T(8,128)S(1)} %bitcast.155, f32[2,8,64]{2,1,0:T(8,128)S(1)} %fusion.4, f32[2,8,64,4,64]{2,4,1,3,0:T(8,128)} %copy-done.1, f32[2,8,64]{2,1,0:T(8,128)S(1)} %get-tuple-element.15, bf16[2,64,8,128,1]{3,2,1,0,4:T(8,128)(2,1)} %bitcast_bitcast_fusion.1, ...), kind=kOutput, calls=%fused_computation.4 | convolution fusion | flops 68681728 | bytes 1978368 | tf_op jit(solution)/shard_map/qthd,cqsd->qhtcs/dot_general | solution.py:100
  56.2 1.5 copy.113
  57.7 16.0 %reduce-scatter.6.cloned.1.call-done = f32[128,128]{1,0:T(8,128)} async-done(((f32[512,128]{1,0:T(8,128)}), f32[128,128]{1,0:T(8,128)}) %reduce-scatter.6.cloned.1.call-update) | async-done | bytes 65552 | tf_op jit(solution)/shard_map/reduce_scatter | solution.py:119
  73.7 0.8 convert_element_type.107
  74.5 0.1 convolution_convert_fusion.5
  74.7 0.6 copy.122
  75.3 4.6 %all-to-all-start.5 = ((bf16[4,32,128]{2,1,0:T(8,128)(2,1)}), bf16[4,32,128]{2,1,0:T(8,128)(2,1)}, u32[]{:S(2)}, u32[]{:S(2)}) async-start(bf16[4,32,128]{2,1,0:T(8,128)(2,1)} %copy.122), calls=%async_computation.7 | async-start | bytes 65536 | tf_op jit(solution)/shard_map/all_to_all | solution.py:126
  79.9 1.7 convolution_bitcast_fusion.4
  81.6 0.7 copy.114
  82.4 3.3 %all-to-all-done.5 = bf16[4,32,128]{2,1,0:T(8,128)(2,1)} async-done(((bf16[4,32,128]{2,1,0:T(8,128)(2,1)}), bf16[4,32,128]{2,1,0:T(8,128)(2,1)}, u32[]{:S(2)}, u32[]{:S(2)}) %all-to-all-start.5) | async-done | bytes 32800 | tf_op jit(solution)/shard_map/all_to_all | solution.py:126
  85.7 1.0 convolution_convert_fusion.4
  86.6 2.7 %convolution_bitcast_fusion = f32[8192,128]{0,1:T(8,128)} fusion(bf16[128,128]{1,0:T(8,128)(2,1)S(1)} %bitcast.143, bf16[128,8192]{1,0:T(8,128)(2,1)S(1)} %copy-done), kind=kOutput, calls=%fused_computation | convolution fusion | flops 268435456 | bytes 6324224 | tf_op jit(solution)/shard_map/tr,th->rh/dot_general | solution.py:134
  89.3 0.5 fusion.11
  89.8 0.2 copy.108
  90.0 0.1 reshape_reshape.7
  90.1 0.3 convolution_convert_fusion.1
  90.4 0.8 copy.110
  91.2 3.4 %all-to-all-start.3 = ((bf16[4,32,1024]{2,1,0:T(8,128)(2,1)}), bf16[4,32,1024]{2,1,0:T(8,128)(2,1)S(1)}, u32[]{:S(2)}, u32[]{:S(2)}) async-start(bf16[4,32,1024]{2,1,0:T(8,128)(2,1)} %copy.110), calls=%async_computation.3 | async-start | bytes 524288 | tf_op jit(solution)/shard_map/all_to_all | solution.py:122
  94.6 9.8 %reduce-scatter.4.cloned.1.call-done = f32[128,128]{1,0:T(8,128)} async-done(((f32[512,128]{1,0:T(8,128)}), f32[128,128]{1,0:T(8,128)}) %reduce-scatter.4.cloned.1.call-update) | async-done | bytes 65552 | tf_op jit(solution)/shard_map/reduce_scatter | solution.py:118
  104.4 0.8 convert_element_type.104
  105.3 0.1 convolution_convert_fusion.7
  105.4 0.6 copy.116
  106.1 4.6 %all-to-all-start.4 = ((bf16[4,32,128]{2,1,0:T(8,128)(2,1)}), bf16[4,32,128]{2,1,0:T(8,128)(2,1)S(1)}, u32[]{:S(2)}, u32[]{:S(2)}) async-start(bf16[4,32,128]{2,1,0:T(8,128)(2,1)} %copy.116), calls=%async_computation.5 | async-start | bytes 65536 | tf_op jit(solution)/shard_map/all_to_all | solution.py:123
  110.6 0.3 convolution_convert_fusion
  111.0 0.8 copy.112
  111.8 4.5 %all-to-all-done.4 = bf16[4,32,128]{2,1,0:T(8,128)(2,1)S(1)} async-done(((bf16[4,32,128]{2,1,0:T(8,128)(2,1)}), bf16[4,32,128]{2,1,0:T(8,128)(2,1)S(1)}, u32[]{:S(2)}, u32[]{:S(2)}) %all-to-all-start.4) | async-done | bytes 32800 | tf_op jit(solution)/shard_map/all_to_all | solution.py:123
  116.3 0.2 convolution_convert_fusion.6
  116.5 0.6 copy.118
  117.1 63.6 %reduce-scatter.8.cloned.1.call-done = f32[512,128]{0,1:T(8,128)} async-done(((f32[8192,128]{0,1:T(8,128)}), f32[512,128]{0,1:T(8,128)}) %reduce-scatter.8.cloned.1.call-update) | async-done | bytes 262160 | tf_op jit(solution)/shard_map/reduce_scatter | solution.py:133
  180.7 1.8 copy.125
  (47 shorter events, 0.9 us)
Async XLA Ops:
  7.2 1.6 copy-start
  8.8 12.4 %copy-start.9 = (s32[4]{0:T(128)}, s32[4]{0:T(128)S(1)}, u32[]{:S(2)}) copy-start(s32[4]{0:T(128)S(1)} %dynamic-slice_bitcast_fusion) | copy-start | bytes 52
  8.8 9.6 %copy-start.5 = (s32[4,1,4]{2,1,0:T(1,128)S(1)}, s32[4,1,4]{2,1,0:T(1,128)}, u32[]{:S(2)}) copy-start(s32[4,1,4]{2,1,0:T(1,128)} %param.13) | copy-start | bytes 196
  8.8 10.0 %copy-start.6 = (s32[2,3]{1,0:T(2,128)S(1)}, s32[2,3]{1,0:T(2,128)}, u32[]{:S(2)}) copy-start(s32[2,3]{1,0:T(2,128)} %param.12) | copy-start | bytes 76
  8.8 10.6 %copy-start.8 = (bf16[128,128]{1,0:T(8,128)(2,1)S(1)}, bf16[128,128]{1,0:T(8,128)(2,1)}, u32[]{:S(2)}) copy-start(bf16[128,128]{1,0:T(8,128)(2,1)} %param.10) | copy-start | bytes 98308
  8.8 10.9 %copy-start.3 = (bf16[128,1024]{1,0:T(8,128)(2,1)S(1)}, bf16[128,1024]{1,0:T(8,128)(2,1)}, u32[]{:S(2)}) copy-start(bf16[128,1024]{1,0:T(8,128)(2,1)} %param.11) | copy-start | bytes 786436
  8.8 12.4 %copy-start.7 = (bf16[128,1024]{1,0:T(8,128)(2,1)S(1)}, bf16[128,1024]{1,0:T(8,128)(2,1)}, u32[]{:S(2)}) copy-start(bf16[128,1024]{1,0:T(8,128)(2,1)} %param.9) | copy-start | bytes 786436
  12.1 12.0 %all-to-all-start.2 = ((bf16[4,32,128]{2,1,0:T(8,128)(2,1)}), bf16[4,32,128]{2,1,0:T(8,128)(2,1)S(1)}, u32[]{:S(2)}, u32[]{:S(2)}) async-start(bf16[4,32,128]{2,1,0:T(8,128)(2,1)} %copy.97), calls=%async_computation.2 | async-start | bytes 65536 | tf_op jit(solution)/shard_map/all_to_all | solution.py:59
  19.8 0.7 copy-start.2
  24.0 9.1 %all-to-all-start = ((bf16[4,32,128]{2,1,0:T(8,128)(2,1)}), bf16[4,32,128]{2,1,0:T(8,128)(2,1)S(1)}, u32[]{:S(2)}, u32[]{:S(2)}) async-start(bf16[4,32,128]{2,1,0:T(8,128)(2,1)} %copy.81), calls=%async_computation | async-start | bytes 65536 | tf_op jit(solution)/shard_map/all_to_all | solution.py:58
  27.6 21.9 %copy-start.11 = (pred[4,4,1]{0,1,2:T(4,128)(4,1)}, pred[4,4,1]{0,1,2:T(4,128)(4,1)S(1)}, u32[]{:S(2)}) copy-start(pred[4,4,1]{0,1,2:T(4,128)(4,1)S(1)} %fusion.40) | copy-start | bytes 52
  33.2 15.2 %all-to-all-start.1 = ((bf16[4,32,1024]{2,1,0:T(8,128)(2,1)}), bf16[4,32,1024]{2,1,0:T(8,128)(2,1)S(1)}, u32[]{:S(2)}, u32[]{:S(2)}) async-start(bf16[4,32,1024]{2,1,0:T(8,128)(2,1)} %copy.89), calls=%async_computation.1 | async-start | bytes 524288 | tf_op jit(solution)/shard_map/all_to_all | solution.py:57
  36.6 37.1 %reduce-scatter.6.cloned.1.call-start = ((), (), s32[]{:S(2)}) async-start(), calls=%async_computation.10 | async-start | bytes 327680 | tf_op jit(solution)/shard_map/reduce_scatter | solution.py:119
  49.4 1.3 copy-start.1
  49.8 1.2 copy-start.4
  56.2 18.3 %copy-start.12 = (pred[4,4,1]{0,1,2:T(4,128)(4,1)S(1)}, pred[4,4,1]{0,1,2:T(4,128)(4,1)}, u32[]{:S(2)}) copy-start(pred[4,4,1]{0,1,2:T(4,128)(4,1)} %copy-done.11) | copy-start | bytes 52
  56.2 29.4 %copy-start.10 = (s32[4]{0:T(128)S(1)}, s32[4]{0:T(128)}, u32[]{:S(2)}) copy-start(s32[4]{0:T(128)} %copy-done.9) | copy-start | bytes 52
  75.3 10.4 %all-to-all-start.5 = ((bf16[4,32,128]{2,1,0:T(8,128)(2,1)}), bf16[4,32,128]{2,1,0:T(8,128)(2,1)}, u32[]{:S(2)}, u32[]{:S(2)}) async-start(bf16[4,32,128]{2,1,0:T(8,128)(2,1)} %copy.122), calls=%async_computation.7 | async-start | bytes 65536 | tf_op jit(solution)/shard_map/all_to_all | solution.py:126
  79.9 24.5 %reduce-scatter.4.cloned.1.call-start = ((), (), s32[]{:S(2)}) async-start(), calls=%async_computation.9 | async-start | bytes 327680 | tf_op jit(solution)/shard_map/reduce_scatter | solution.py:118
  82.3 98.4 %reduce-scatter.8.cloned.1.call-start = ((), (), s32[]{:S(2)}) async-start(), calls=%async_computation.11 | async-start | bytes 4456448 | tf_op jit(solution)/shard_map/reduce_scatter | solution.py:133
  91.2 14.9 %all-to-all-start.3 = ((bf16[4,32,1024]{2,1,0:T(8,128)(2,1)}), bf16[4,32,1024]{2,1,0:T(8,128)(2,1)S(1)}, u32[]{:S(2)}, u32[]{:S(2)}) async-start(bf16[4,32,1024]{2,1,0:T(8,128)(2,1)} %copy.110), calls=%async_computation.3 | async-start | bytes 524288 | tf_op jit(solution)/shard_map/all_to_all | solution.py:122
  106.1 10.2 %all-to-all-start.4 = ((bf16[4,32,128]{2,1,0:T(8,128)(2,1)}), bf16[4,32,128]{2,1,0:T(8,128)(2,1)S(1)}, u32[]{:S(2)}, u32[]{:S(2)}) async-start(bf16[4,32,128]{2,1,0:T(8,128)(2,1)} %copy.116), calls=%async_computation.5 | async-start | bytes 65536 | tf_op jit(solution)/shard_map/all_to_all | solution.py:123
Sparse Core Ops, SparseCore 0:
  52.2 21.4 reduce-scatter.5
  83.9 20.5 reduce-scatter.3
  108.3 72.3 reduce-scatter.7
where the time goes:
time: 190 us; the launch traced here: 189 us
  waiting for transfers between devices  104 us (55%)
  starting transfers between devices  25.9 us (14%)
  matrix products  16 us (8%)
  local copies, waits for them, and re-layouts  14.7 us (8%)
  between operations  14.1 us (7%)
  blocking collectives  11.3 us (6%)
  other arithmetic  3.44 us (2%)
    reduce_scatter x1, waiting for transfers between devices, local(): lax.psum_scatter(jnp.einsum('tr,th->rh', inputs, value_grad, preferred_el...  63.6 us
    reduce_scatter x1, waiting for transfers between devices, local(): lax.psum_scatter(value_total, 'ctx', scatter_dimension=0, tiled=True)  16 us
    reduce_scatter x1, waiting for transfers between devices, local(): lax.psum_scatter(key_total, 'ctx', scatter_dimension=0, tiled=True)  9.85 us
    all_to_all x1, starting transfers between devices, local(): lax.all_to_all(pack_out(values), 'dp', split_axis=0, concat_axis=0, tiled...  6.32 us
    all_gather x1, blocking collectives, local(): lax.all_gather(value_rows, 'ctx', axis=0, tiled=True)  5.86 us
    all_gather x1, blocking collectives, local(): lax.all_gather(key_rows, 'ctx', axis=0, tiled=True)  5.43 us
    all_to_all x1, waiting for transfers between devices, local(): lax.all_to_all(pack_out(keys), 'dp', split_axis=0, concat_axis=0, tiled=T...  4.8 us
    all_to_all x1, starting transfers between devices, local(): lax.all_to_all(pack_back(value_own.astype(jnp.bfloat16)), 'dp', split_axi...  4.59 us
  transfers between devices with their start and end apart: 9, of which 7 were waited for; matrix products, arithmetic and copies ran while one was open for 11% of the time, Pallas kernels for 0%

commit v1 on v0

v1 whole, which is shorter than its diff:
```python
import functools
import math

import jax
import jax.numpy as jnp
from jax import lax
from jax.experimental import pallas as pl
from jax.experimental.pallas import tpu as pltpu
from jax.sharding import PartitionSpec as P

TILE = 16
CHUNKS = 4
BF16 = jnp.bfloat16
F32 = jnp.float32
KV, Q, DQ, DKV, WG = range(5)
GATHER, REDUCE, VGRAD = range(3)


def contract_rows(left, right):
    return lax.dot_general(left, right, (((0,), (0,)), ((), ())), preferred_element_type=F32)


def contract_lanes(left, right):
    return lax.dot_general(left, right, (((1,), (1,)), ((), ())), preferred_element_type=F32)


def pick(flags, pieces):
    total = flags[0] * pieces[0].astype(F32)
    for flag, piece in zip(flags[1:], pieces[1:]):
        total = total + flag * piece.astype(F32)
    return total.astype(BF16)


def kernel(
    data, ctx, x_ref, cols_ref, w_ref, q_ref, k_ref, g_ref, doc_ref, route_ref,
    qg_ref, kg_ref, wg_ref,
    x_buf, w_buf, kv_send, kv_recv, q_send, q_recv, kv_all, x_recv,
    red_send, red_recv, dq_send, dq_recv, dkv_send, dkv_recv, vg_all, wg_send, wg_recv,
    load_sem, own_sem, dp_send_sem, dp_recv_sem, ctx_send_sem, ctx_recv_sem, x_send_sem, x_recv_sem,
):
    rank, col = lax.axis_index("dp"), lax.axis_index("ctx")
    rows, head = k_ref.shape
    width = q_ref.shape[1]
    heads = width // head
    groups = route_ref.shape[1]
    size = rows // groups
    packs, docs = doc_ref.shape
    seg = rows // packs
    block = wg_ref.shape[0]
    depth = x_ref.shape[1]
    step = depth // CHUNKS
    direct = groups == data
    aligned = block % 128 == 0
    ranks = [lax.rem(rank + i, data) for i in range(data)]
    cols = [lax.rem(col + i, ctx) for i in range(ctx)]

    def to_rank(phase, i, src, dst):
        return pltpu.make_async_remote_copy(
            src_ref=src, dst_ref=dst, send_sem=dp_send_sem.at[phase, i],
            recv_sem=dp_recv_sem.at[phase, i], device_id={"dp": ranks[i]},
            device_id_type=pl.DeviceIdType.MESH)

    def to_col(phase, i, src, dst):
        return pltpu.make_async_remote_copy(
            src_ref=src, dst_ref=dst, send_sem=ctx_send_sem.at[phase, i],
            recv_sem=ctx_recv_sem.at[phase, i], device_id={"ctx": cols[i]},
            device_id_type=pl.DeviceIdType.MESH)

    barrier = pltpu.get_barrier_semaphore()
    for i in range(1, data):
        pl.semaphore_signal(barrier, inc=1, device_id={"dp": ranks[i]}, device_id_type=pl.DeviceIdType.MESH)
    for i in range(1, ctx):
        pl.semaphore_signal(barrier, inc=1, device_id={"ctx": cols[i]}, device_id_type=pl.DeviceIdType.MESH)

    loads = []
    for n in range(CHUNKS):
        span = pl.ds(n * step, step)
        loads.append((
            pltpu.make_async_copy(x_ref.at[:, span], x_buf.at[:, span], load_sem.at[0, n]),
            pltpu.make_async_copy(w_ref.at[span, :], w_buf.at[span, :], load_sem.at[1, n])))
        for load in loads[-1]:
            load.start()

    going = [[(route_ref[rank, j] == ranks[i]).astype(F32) for j in range(groups)] for i in range(data)]
    if not direct:
        placed, before = [], 0
        for s in range(data):
            count = 0
            for j in range(groups):
                count = count + (route_ref[s, j] == rank).astype(jnp.int32)
            placed.append([((before == k) & (count > 0)).astype(F32) for k in range(groups)])
            before = before + count

    def parts(array):
        return [array[j * size:(j + 1) * size] for j in range(groups)]

    q_parts, k_parts = parts(q_ref[...]), parts(k_ref[...])
    for i in range(data):
        piece = pick(going[i], q_parts)
        if i == 0:
            q_recv[rank] = piece
        else:
            q_send[i] = piece
    values = jnp.zeros((rows, head), F32)
    for n in range(CHUNKS):
        for load in loads[n]:
            load.wait()
        values = values + jnp.dot(
            x_buf[:, n * step:(n + 1) * step], w_buf[n * step:(n + 1) * step, :],
            preferred_element_type=F32)
    v_parts = parts(values.astype(BF16))
    for i in range(data):
        piece = jnp.concatenate([pick(going[i], k_parts), pick(going[i], v_parts)], axis=1)
        if i == 0:
            kv_recv[rank] = piece
        else:
            kv_send[i] = piece

    pl.semaphore_wait(barrier, data - 1 + ctx - 1)

    kv_out = [to_rank(KV, i, kv_send.at[i], kv_recv.at[rank]) for i in range(1, data)]
    q_out = [to_rank(Q, i, q_send.at[i], q_recv.at[rank]) for i in range(1, data)]
    for copy in kv_out + q_out:
        copy.start()
    x_out, x_own = [], []
    for d in range(data if aligned else 1):
        for i in range(ctx):
            if aligned:
                start = pl.multiple_of((d * ctx + cols[i]) * block, block)
                source = x_buf.at[:, pl.ds(start, block)]
            else:
                source = cols_ref.at[cols[i]]
            if i == 0:
                x_own.append(pltpu.make_async_copy(source, x_recv.at[d, col], own_sem.at[d]))
            else:
                x_out.append(pltpu.make_async_remote_copy(
                    src_ref=source, dst_ref=x_recv.at[d, col],
                    send_sem=x_send_sem.at[d, i], recv_sem=x_recv_sem.at[d, i],
                    device_id={"ctx": cols[i]}, device_id_type=pl.DeviceIdType.MESH))
    for copy in x_own:
        copy.start()

    def arrange(buffer):
        if direct:
            return buffer[...].reshape(rows, buffer.shape[2])
        pieces = [buffer[s] for s in range(data)]
        return jnp.concatenate(
            [pick([placed[s][k] for s in range(data)], pieces) for k in range(groups)], axis=0)

    for copy in kv_out:
        copy.wait_recv()
    kv_all[col] = arrange(kv_recv)
    gather = [to_col(GATHER, i, kv_all.at[col], kv_all.at[col]) for i in range(1, ctx)]
    for copy in gather:
        copy.start()
    for copy in x_out:
        copy.start()
    for copy in q_out:
        copy.wait_recv()
    queries = arrange(q_recv)
    for copy in gather:
        copy.wait_recv()

    scale = 1.0 / math.sqrt(head)
    pack_len = ctx * seg

    def stack(array, p):
        return jnp.concatenate(
            [array[p * seg:(p + 1) * seg, h * head:(h + 1) * head] for h in range(heads)], axis=0)

    scores_grad, query_stacks, key_stacks = [], [], []
    for p in range(packs):
        pair = kv_all[:, p * seg:(p + 1) * seg, :].reshape(pack_len, 2 * head)
        keys, vals = pair[:, :head], pair[:, head:]
        query_pos = col * seg + lax.broadcasted_iota(jnp.int32, (seg, pack_len), 0)
        key_pos = lax.broadcasted_iota(jnp.int32, (seg, pack_len), 1)
        query_doc, key_doc, end = jnp.zeros_like(query_pos), jnp.zeros_like(key_pos), 0
        for n in range(docs):
            end = end + doc_ref[p, n] * TILE
            query_doc = query_doc + jnp.where(query_pos >= end, 1, 0)
            key_doc = key_doc + jnp.where(key_pos >= end, 1, 0)
        bias = jnp.where((query_doc == key_doc) & (key_pos <= query_pos), 0.0, -1e30)
        query_stack, grad_stack = stack(queries, p), stack(g_ref, p)
        scores = contract_lanes(query_stack, keys) * scale
        scores = (scores.reshape(heads, seg, pack_len) + bias[None]).reshape(heads * seg, pack_len)
        weights = jnp.exp(scores - jnp.max(scores, axis=1, keepdims=True))
        probs = weights * (1.0 / jnp.sum(weights, axis=1, keepdims=True))
        grad_probs = contract_lanes(grad_stack, vals)
        inner = jnp.sum(probs * grad_probs, axis=1, keepdims=True)
        ds = (probs * (grad_probs - inner) * scale).astype(BF16)
        dk = contract_rows(ds, query_stack).astype(BF16)
        dv = contract_rows(probs.astype(BF16), grad_stack).astype(BF16)
        red_send[:, p * seg:(p + 1) * seg, :head] = dk.reshape(ctx, seg, head)
        red_send[:, p * seg:(p + 1) * seg, head:] = dv.reshape(ctx, seg, head)
        scores_grad.append(ds)
        key_stacks.append(keys)
    reduce = [to_col(REDUCE, i, red_send.at[cols[i]], red_recv.at[i]) for i in range(1, ctx)]
    for copy in reduce:
        copy.start()

    halves = []
    for p in range(packs):
        dq = jnp.dot(scores_grad[p], key_stacks[p], preferred_element_type=F32).astype(BF16)
        halves.append(jnp.concatenate([dq[h * seg:(h + 1) * seg] for h in range(heads)], axis=1))
    dq_rows = jnp.concatenate(halves, axis=0)

    def hand_back(array, send, recv, phase):
        if direct:
            send[...] = array.reshape(send.shape)
            recv[rank] = send[rank]
            copies = [to_rank(phase, i, send.at[ranks[i]], recv.at[rank]) for i in range(1, data)]
        else:
            pieces = parts(array)
            for s in range(data):
                send[s] = pick(placed[s], pieces)
            recv[rank] = send[rank]
            copies = [to_rank(phase, i, send.at[ranks[i]], recv.at[rank]) for i in range(1, data)]
        for copy in copies:
            copy.start()
        return copies

    def restore(recv):
        pieces = [recv[ranks[i]] for i in range(data)]
        return jnp.concatenate(
            [pick([going[i][j] for i in range(data)], pieces) for j in range(groups)], axis=0)

    dq_out = hand_back(dq_rows, dq_send, dq_recv, DQ)

    total = red_send[col].astype(F32)
    for copy in reduce:
        copy.wait_recv()
    for i in range(1, ctx):
        total = total + red_recv[i].astype(F32)
    dkv_out = hand_back(total.astype(BF16), dkv_send, dkv_recv, DKV)
    for copy in dkv_out:
        copy.wait_recv()
    dkv = restore(dkv_recv)
    vg_all[col] = dkv[:, head:]
    vgrad = [to_col(VGRAD, i, vg_all.at[col], vg_all.at[col]) for i in range(1, ctx)]
    for copy in vgrad:
        copy.start()
    kg_ref[...] = dkv[:, :head]
    for copy in x_out:
        copy.wait_recv()
    for copy in x_own:
        copy.wait()
    for copy in vgrad:
        copy.wait_recv()
    value_grad = vg_all[...].reshape(ctx * rows, head)
    wg_out = []
    if not aligned:
        terms = contract_rows(x_recv[0].reshape(ctx * rows, data * block), value_grad)
        wg_send[...] = terms.astype(BF16).reshape(wg_send.shape)
    for i in range(1, data):
        if aligned:
            term = contract_rows(value_grad, x_recv[ranks[i]].reshape(ctx * rows, block))
            wg_send[ranks[i]] = term.astype(BF16)
        copy = to_rank(WG, i, wg_send.at[ranks[i]], wg_recv.at[i])
        copy.start()
        wg_out.append(copy)
    if aligned:
        weight_grad = contract_rows(value_grad, x_recv[rank].reshape(ctx * rows, block))
    else:
        weight_grad = wg_send[rank].astype(F32)
    for copy in dq_out:
        copy.wait_recv()
    qg_ref[...] = restore(dq_recv)
    for copy in wg_out:
        copy.wait_recv()
    for i in range(1, data):
        weight_grad = weight_grad + wg_recv[i].astype(F32)
    wg_ref[...] = weight_grad.T if aligned else weight_grad
    for copy in kv_out + q_out + x_out + gather + reduce + dq_out + dkv_out + vgrad + wg_out:
        copy.wait_send()


def local(inputs, value_weight, queries, keys, out_grad, doc_tiles, route):
    data, ctx = lax.axis_size("dp"), lax.axis_size("ctx")
    rows, depth = inputs.shape
    head, width = keys.shape[1], queries.shape[1]
    groups = route.shape[2]
    size = rows // groups
    block = depth // (data * ctx)
    columns, blocks, term = inputs, (data, ctx, rows, block), (data, head, block)
    if block % 128:
        columns = jnp.transpose(inputs.reshape(rows, data, ctx, block), (2, 0, 1, 3))
        columns = columns.reshape(ctx, rows, data * block)
        blocks, term = (1, ctx, rows, data * block), (data, block, head)
    vmem = pl.BlockSpec(memory_space=pltpu.VMEM)
    smem = pl.BlockSpec(memory_space=pltpu.SMEM)
    anywhere = pl.BlockSpec(memory_space=pl.ANY)
    dma = pltpu.SemaphoreType.DMA
    return pl.pallas_call(
        functools.partial(kernel, data, ctx),
        out_shape=(
            jax.ShapeDtypeStruct((rows, width), BF16),
            jax.ShapeDtypeStruct((rows, head), BF16),
            jax.ShapeDtypeStruct((block, head), F32)),
        in_specs=[anywhere, anywhere, anywhere, vmem, vmem, vmem, smem, smem],
        out_specs=(vmem, vmem, vmem),
        scratch_shapes=[
            pltpu.VMEM((rows, depth), BF16),
            pltpu.VMEM((depth, head), BF16),
            pltpu.VMEM((data, size, 2 * head), BF16),
            pltpu.VMEM((data, size, 2 * head), BF16),
            pltpu.VMEM((data, size, width), BF16),
            pltpu.VMEM((data, size, width), BF16),
            pltpu.VMEM((ctx, rows, 2 * head), BF16),
            pltpu.VMEM(blocks, BF16),
            pltpu.VMEM((ctx, rows, 2 * head), BF16),
            pltpu.VMEM((ctx, rows, 2 * head), BF16),
            pltpu.VMEM((data, size, width), BF16),
            pltpu.VMEM((data, size, width), BF16),
            pltpu.VMEM((data, size, 2 * head), BF16),
            pltpu.VMEM((data, size, 2 * head), BF16),
            pltpu.VMEM((ctx, rows, head), BF16),
            pltpu.VMEM(term, BF16),
            pltpu.VMEM(term, BF16),
            dma((2, CHUNKS)), dma((data,)),
            dma((5, data)), dma((5, data)), dma((3, ctx)), dma((3, ctx)),
            dma((data, ctx)), dma((data, ctx)),
        ],
        compiler_params=pltpu.CompilerParams(
            collective_id=0, has_side_effects=True, vmem_limit_bytes=48 * 1024 * 1024),
    )(inputs, columns, value_weight, queries, keys, out_grad, doc_tiles, route[:, 0, :])


def solution(mesh):
    in_specs = (
        P(("dp", "ctx"), None),
        P(None, "tensor"),
        P(("dp", "ctx"), "tensor"),
        P(("dp", "ctx"), "tensor"),
        P(("dp", "ctx"), "tensor"),
        P("dp", None),
        P(None, "ctx", None),
    )
    out_specs = (P(("dp", "ctx"), "tensor"), P(("dp", "ctx"), "tensor"), P(("dp", "ctx"), "tensor"))
    return jax.shard_map(local, mesh=mesh, in_specs=in_specs, out_specs=out_specs, check_vma=False)
```

time: 190 us -> 67.7 us (0.36)
  waiting for transfers between devices: 104 us -> 0 us
  Pallas kernels: 0 us -> 57.5 us
  starting transfers between devices: 25.9 us -> 0 us
  matrix products: 16 us -> 0 us
  between operations: 14.1 us -> 0.66 us
  blocking collectives: 11.3 us -> 0 us
  local copies, waits for them, and re-layouts: 14.7 us -> 9.21 us
  other arithmetic: 3.44 us -> 0 us
    reduce_scatter x3 -> x0, waiting for transfers between devices: 89.4 us -> none  [the longest x1 63.6 us: local(): lax.psum_scatter(jnp.einsum('tr,th->rh', inputs, value_grad, preferred_el...]
    pallas_call x0 -> x1, Pallas kernels: none -> 57.5 us  [local(): pl.pallas_call(functools.partial(kernel, data, ctx), out_shape=(jax.Shape...]
    all_to_all x6 -> x0, starting transfers between devices: 25.8 us -> none  [the longest x1 6.32 us: local(): lax.all_to_all(pack_out(values), 'dp', split_axis=0, concat_axis=0, tiled...]
    dot_general x20 -> x0, matrix products: 16 us -> none  [the longest x1 2.67 us: local(): jnp.einsum('tr,th->rh', inputs, value_grad, preferred_element_type=jnp.fl...]
    all_to_all x6 -> x0, waiting for transfers between devices: 14.2 us -> none  [the longest x1 4.8 us: local(): lax.all_to_all(pack_out(keys), 'dp', split_axis=0, concat_axis=0, tiled=T...]
    all_gather x2 -> x0, blocking collectives: 11.3 us -> none  [the longest x1 5.86 us: local(): lax.all_gather(value_rows, 'ctx', axis=0, tiled=True)]
    convert_element_type x14 -> x0, local copies, waits for them, and re-layouts: 7.22 us -> none  [the longest x3 2.04 us: pack_back(): outbound.astype(jnp.bfloat16)]
    unnamed x29 -> x17, local copies, waits for them, and re-layouts: 4.17 us -> 9.21 us
  transfers between devices with their start and end apart: 9 -> 0, of which waited for: 7 -> 0; matrix products, arithmetic and copies ran while one was open for 11% -> 0% of each run, Pallas kernels for 0% -> 0%
where the time goes in v1:
time: 67.7 us; the launch traced here: 67.4 us
  Pallas kernels  57.5 us (85%)
  local copies, waits for them, and re-layouts  9.21 us (14%)
    pallas_call x1, Pallas kernels, local(): pl.pallas_call(functools.partial(kernel, data, ctx), out_shape=(jax.Shape...  57.5 us
    unnamed x17, local copies, waits for them, and re-layouts  9.21 us

profile of v1, /device:TPU:0, one launch (start us, length us, event | category | flops | bytes accessed | tf_op | source)
XLA Modules:
  0.0 67.4 jit_solution(15097078758151486247)
XLA Ops:
  0.6 0.0 copy-start
  0.6 1.6 %copy-done = bf16[128,8192]{1,0:T(8,128)(2,1)S(1)} copy-done((bf16[128,8192]{1,0:T(8,128)(2,1)S(1)}, bf16[128,8192]{1,0:T(8,128)(2,1)}, u32[]{:S(2)}) %copy-start) | copy-done | bytes 2097176
  2.2 0.0 copy-start.1
  2.2 1.6 %copy-done.1 = bf16[8192,128]{1,0:T(8,128)(2,1)S(1)} copy-done((bf16[8192,128]{1,0:T(8,128)(2,1)S(1)}, bf16[8192,128]{1,0:T(8,128)(2,1)}, u32[]{:S(2)}) %copy-start.1) | copy-done | bytes 2097176
  3.8 0.0 copy-start.2
  3.8 0.9 %copy-done.2 = bf16[128,1024]{1,0:T(8,128)(2,1)S(1)} copy-done((bf16[128,1024]{1,0:T(8,128)(2,1)S(1)}, bf16[128,1024]{1,0:T(8,128)(2,1)}, u32[]{:S(2)}) %copy-start.2) | copy-done | bytes 262168
  4.8 0.0 copy-start.3
  4.8 0.9 %copy-done.3 = bf16[128,1024]{1,0:T(8,128)(2,1)S(1)} copy-done((bf16[128,1024]{1,0:T(8,128)(2,1)S(1)}, bf16[128,1024]{1,0:T(8,128)(2,1)}, u32[]{:S(2)}) %copy-start.3) | copy-done | bytes 262168
  5.7 0.0 copy-start.4
  5.7 0.8 %copy-done.4 = bf16[128,128]{1,0:T(8,128)(2,1)S(1)} copy-done((bf16[128,128]{1,0:T(8,128)(2,1)S(1)}, bf16[128,128]{1,0:T(8,128)(2,1)}, u32[]{:S(2)}) %copy-start.4) | copy-done | bytes 32792
  6.5 0.0 copy-start.5
  6.5 0.7 %copy-done.5 = s32[4,1,4]{2,1,0:T(1,128)S(1)} copy-done((s32[4,1,4]{2,1,0:T(1,128)S(1)}, s32[4,1,4]{2,1,0:T(1,128)}, u32[]{:S(2)}) %copy-start.5) | copy-done | bytes 88
  7.2 0.0 copy-start.6
  7.2 0.7 %copy-done.6 = s32[2,3]{1,0:T(2,128)S(1)} copy-done((s32[2,3]{1,0:T(2,128)S(1)}, s32[2,3]{1,0:T(2,128)}, u32[]{:S(2)}) %copy-start.6) | copy-done | bytes 48
  7.8 57.5 %shard_map.94 = (bf16[128,1024]{1,0:T(8,128)(2,1)S(1)}, bf16[128,128]{1,0:T(8,128)(2,1)S(1)}, f32[512,128]{1,0:T(8,128)S(1)}) custom-call(bf16[128,8192]{1,0:T(8,128)(2,1)S(1)} %copy-done, bf16[128,8192]{1,0:T(8,128)(2,1)S(1)} %copy-done, bf16[8192,128]{1,0:T(8,128)(2,1)S(1)} %copy-done.1, bf16[128,1024]{1,0:T(8,128)(2,1)S(1)} %copy-done.2, ...), custom_call_target="tpu_custom_call" | custom-call | tf_op jit(solution)/shard_map/pallas_call | solution.py:293
  65.3 0.7 %copy.13 = bf16[128,1024]{1,0:T(8,128)(2,1)} copy(bf16[128,1024]{1,0:T(8,128)(2,1)S(1)} %get-tuple-element.6) | data formatting | bytes 524288
  66.1 0.6 copy.14
  66.7 0.7 %copy.15 = f32[512,128]{1,0:T(8,128)} copy(f32[512,128]{1,0:T(8,128)S(1)} %get-tuple-element.8) | data formatting | bytes 524288
Async XLA Ops:
  0.6 1.6 %copy-start = (bf16[128,8192]{1,0:T(8,128)(2,1)S(1)}, bf16[128,8192]{1,0:T(8,128)(2,1)}, u32[]{:S(2)}) copy-start(bf16[128,8192]{1,0:T(8,128)(2,1)} %cols_ref.1) | copy-start | bytes 6291460
  2.2 1.6 %copy-start.1 = (bf16[8192,128]{1,0:T(8,128)(2,1)S(1)}, bf16[8192,128]{1,0:T(8,128)(2,1)}, u32[]{:S(2)}) copy-start(bf16[8192,128]{1,0:T(8,128)(2,1)} %w_ref.1) | copy-start | bytes 6291460
  3.8 0.9 %copy-start.2 = (bf16[128,1024]{1,0:T(8,128)(2,1)S(1)}, bf16[128,1024]{1,0:T(8,128)(2,1)}, u32[]{:S(2)}) copy-start(bf16[128,1024]{1,0:T(8,128)(2,1)} %q_ref.1) | copy-start | bytes 786436
  4.8 0.9 %copy-start.3 = (bf16[128,1024]{1,0:T(8,128)(2,1)S(1)}, bf16[128,1024]{1,0:T(8,128)(2,1)}, u32[]{:S(2)}) copy-start(bf16[128,1024]{1,0:T(8,128)(2,1)} %g_ref.1) | copy-start | bytes 786436
  5.7 0.8 %copy-start.4 = (bf16[128,128]{1,0:T(8,128)(2,1)S(1)}, bf16[128,128]{1,0:T(8,128)(2,1)}, u32[]{:S(2)}) copy-start(bf16[128,128]{1,0:T(8,128)(2,1)} %k_ref.1) | copy-start | bytes 98308
  6.5 0.7 %copy-start.5 = (s32[4,1,4]{2,1,0:T(1,128)S(1)}, s32[4,1,4]{2,1,0:T(1,128)}, u32[]{:S(2)}) copy-start(s32[4,1,4]{2,1,0:T(1,128)} %param.13) | copy-start | bytes 196
  7.2 0.7 %copy-start.6 = (s32[2,3]{1,0:T(2,128)S(1)}, s32[2,3]{1,0:T(2,128)}, u32[]{:S(2)}) copy-start(s32[2,3]{1,0:T(2,128)} %doc_ref.1) | copy-start | bytes 76

commit v2 on v1

--- a/solution.py
+++ b/solution.py
@@ -32,17 +32,17 @@
 
 
 def kernel(
-    data, ctx, x_ref, cols_ref, w_ref, q_ref, k_ref, g_ref, doc_ref, route_ref,
+    data, ctx, x_ref, cols_ref, w_ref, q_hbm, k_hbm, g_hbm, doc_hbm, route_hbm,
     qg_ref, kg_ref, wg_ref,
-    x_buf, w_buf, kv_send, kv_recv, q_send, q_recv, kv_all, x_recv,
+    x_buf, w_buf, q_ref, k_ref, g_ref, doc_ref, route_ref, kv_send, kv_recv, q_send, q_recv, kv_all, x_recv,
     red_send, red_recv, dq_send, dq_recv, dkv_send, dkv_recv, vg_all, wg_send, wg_recv,
-    load_sem, own_sem, dp_send_sem, dp_recv_sem, ctx_send_sem, ctx_recv_sem, x_send_sem, x_recv_sem,
+    load_sem, small_sem, own_sem, dp_send_sem, dp_recv_sem, ctx_send_sem, ctx_recv_sem, x_send_sem, x_recv_sem,
 ):
     rank, col = lax.axis_index("dp"), lax.axis_index("ctx")
     rows, head = k_ref.shape
     width = q_ref.shape[1]
     heads = width // head
-    groups = route_ref.shape[1]
+    groups = route_ref.shape[2]
     size = rows // groups
     packs, docs = doc_ref.shape
     seg = rows // packs
@@ -72,6 +72,12 @@
     for i in range(1, ctx):
         pl.semaphore_signal(barrier, inc=1, device_id={"ctx": cols[i]}, device_id_type=pl.DeviceIdType.MESH)
 
+    small = [
+        pltpu.make_async_copy(src, dst, small_sem.at[n])
+        for n, (src, dst) in enumerate((
+            (route_hbm, route_ref), (doc_hbm, doc_ref), (k_hbm, k_ref), (q_hbm, q_ref), (g_hbm, g_ref)))]
+    for copy in small:
+        copy.start()
     loads = []
     for n in range(CHUNKS):
         span = pl.ds(n * step, step)
@@ -81,26 +87,43 @@
         for load in loads[-1]:
             load.start()
 
-    going = [[(route_ref[rank, j] == ranks[i]).astype(F32) for j in range(groups)] for i in range(data)]
+    pl.semaphore_wait(barrier, data - 1 + ctx - 1)
+
+    x_out, x_own = [], []
+    for d in range(data if aligned else 1):
+        for i in range(ctx):
+            if aligned:
+                start = pl.multiple_of((d * ctx + cols[i]) * block, block)
+                source = x_ref.at[:, pl.ds(start, block)]
+            else:
+                source = cols_ref.at[cols[i]]
+            if i == 0:
+                x_own.append(pltpu.make_async_copy(source, x_recv.at[d, col], own_sem.at[d]))
+            else:
+                x_out.append(pltpu.make_async_remote_copy(
+                    src_ref=source, dst_ref=x_recv.at[d, col],
+                    send_sem=x_send_sem.at[d, i], recv_sem=x_recv_sem.at[d, i],
+                    device_id={"ctx": cols[i]}, device_id_type=pl.DeviceIdType.MESH))
+    for copy in x_own + x_out:
+        copy.start()
+
+    for copy in small[:3]:
+        copy.wait()
+
+    going = [[(route_ref[rank, 0, j] == ranks[i]).astype(F32) for j in range(groups)] for i in range(data)]
     if not direct:
         placed, before = [], 0
         for s in range(data):
             count = 0
             for j in range(groups):
-                count = count + (route_ref[s, j] == rank).astype(jnp.int32)
+                count = count + (route_ref[s, 0, j] == rank).astype(jnp.int32)
             placed.append([((before == k) & (count > 0)).astype(F32) for k in range(groups)])
             before = before + count
 
     def parts(array):
         return [array[j * size:(j + 1) * size] for j in range(groups)]
 
-    q_parts, k_parts = parts(q_ref[...]), parts(k_ref[...])
-    for i in range(data):
-        piece = pick(going[i], q_parts)
-        if i == 0:
-            q_recv[rank] = piece
-        else:
-            q_send[i] = piece
+    k_parts = parts(k_ref[...])
     values = jnp.zeros((rows, head), F32)
     for n in range(CHUNKS):
         for load in loads[n]:
@@ -116,30 +139,17 @@
         else:
             kv_send[i] = piece
 
-    pl.semaphore_wait(barrier, data - 1 + ctx - 1)
-
     kv_out = [to_rank(KV, i, kv_send.at[i], kv_recv.at[rank]) for i in range(1, data)]
-    q_out = [to_rank(Q, i, q_send.at[i], q_recv.at[rank]) for i in range(1, data)]
-    for copy in kv_out + q_out:
-        copy.start()
-    x_out, x_own = [], []
-    for d in range(data if aligned else 1):
-        for i in range(ctx):
-            if aligned:
-                start = pl.multiple_of((d * ctx + cols[i]) * block, block)
-                source = x_buf.at[:, pl.ds(start, block)]
-            else:
-                source = cols_ref.at[cols[i]]
-            if i == 0:
-                x_own.append(pltpu.make_async_copy(source, x_recv.at[d, col], own_sem.at[d]))
-            else:
-                x_out.append(pltpu.make_async_remote_copy(
-                    src_ref=source, dst_ref=x_recv.at[d, col],
-                    send_sem=x_send_sem.at[d, i], recv_sem=x_recv_sem.at[d, i],
-                    device_id={"ctx": cols[i]}, device_id_type=pl.DeviceIdType.MESH))
-    for copy in x_own:
-        copy.start()
-
+    for copy in kv_out:
+        copy.start()
+    small[3].wait()
+    q_parts = parts(q_ref[...])
+    q_out = []
+    for i in range(1, data):
+        q_send[i] = pick(going[i], q_parts)
+        q_out.append(to_rank(Q, i, q_send.at[i], q_recv.at[rank]))
+        q_out[-1].start()
+    q_recv[rank] = pick(going[0], q_parts)
     def arrange(buffer):
         if direct:
             return buffer[...].reshape(rows, buffer.shape[2])
@@ -153,8 +163,7 @@
     gather = [to_col(GATHER, i, kv_all.at[col], kv_all.at[col]) for i in range(1, ctx)]
     for copy in gather:
         copy.start()
-    for copy in x_out:
-        copy.start()
+    small[4].wait()
     for copy in q_out:
         copy.wait_recv()
     queries = arrange(q_recv)
@@ -287,8 +296,7 @@
         columns = columns.reshape(ctx, rows, data * block)
         blocks, term = (1, ctx, rows, data * block), (data, block, head)
     vmem = pl.BlockSpec(memory_space=pltpu.VMEM)
-    smem = pl.BlockSpec(memory_space=pltpu.SMEM)
-    anywhere = pl.BlockSpec(memory_space=pl.ANY)
+    hbm = pl.BlockSpec(memory_space=pltpu.HBM)
     dma = pltpu.SemaphoreType.DMA
     return pl.pallas_call(
         functools.partial(kernel, data, ctx),
@@ -296,11 +304,16 @@
             jax.ShapeDtypeStruct((rows, width), BF16),
             jax.ShapeDtypeStruct((rows, head), BF16),
             jax.ShapeDtypeStruct((block, head), F32)),
-        in_specs=[anywhere, anywhere, anywhere, vmem, vmem, vmem, smem, smem],
+        in_specs=[hbm] * 8,
         out_specs=(vmem, vmem, vmem),
         scratch_shapes=[
             pltpu.VMEM((rows, depth), BF16),
             pltpu.VMEM((depth, head), BF16),
+            pltpu.VMEM((rows, width), BF16),
+            pltpu.VMEM((rows, head), BF16),
+            pltpu.VMEM((rows, width), BF16),
+            pltpu.SMEM(doc_tiles.shape, jnp.int32),
+            pltpu.SMEM(route.shape, jnp.int32),
             pltpu.VMEM((data, size, 2 * head), BF16),
             pltpu.VMEM((data, size, 2 * head), BF16),
             pltpu.VMEM((data, size, width), BF16),
@@ -316,13 +329,13 @@
             pltpu.VMEM((ctx, rows, head), BF16),
             pltpu.VMEM(term, BF16),
             pltpu.VMEM(term, BF16),
-            dma((2, CHUNKS)), dma((data,)),
+            dma((2, CHUNKS)), dma((5,)), dma((data,)),
             dma((5, data)), dma((5, data)), dma((3, ctx)), dma((3, ctx)),
             dma((data, ctx)), dma((data, ctx)),
         ],
         compiler_params=pltpu.CompilerParams(
-            collective_id=0, has_side_effects=True, vmem_limit_bytes=48 * 1024 * 1024),
-    )(inputs, columns, value_weight, queries, keys, out_grad, doc_tiles, route[:, 0, :])
+            collective_id=0, has_side_effects=True, vmem_limit_bytes=65000 * 1024),
+    )(inputs, columns, value_weight, queries, keys, out_grad, doc_tiles, route)
 
 
 def solution(mesh):

time: 67.7 us -> 64.4 us (0.951)
  local copies, waits for them, and re-layouts: 9.21 us -> 4.71 us
  Pallas kernels: 57.5 us -> 58.8 us
    unnamed x17 -> x3, local copies, waits for them, and re-layouts: 9.21 us -> 4.71 us
    pallas_call x1, Pallas kernels: 57.5 us -> 58.8 us  [local(): pl.pallas_call(functools.partial(kernel, data, ctx), out_shape=(jax.Shape...]
where the time goes in v2:
time: 64.4 us; the launch traced here: 64.2 us
  Pallas kernels  58.8 us (91%)
  local copies, waits for them, and re-layouts  4.71 us (7%)
    pallas_call x1, Pallas kernels, local(): pl.pallas_call(functools.partial(kernel, data, ctx), out_shape=(jax.Shape...  58.8 us
    unnamed x3, local copies, waits for them, and re-layouts  4.71 us

profile of v2, /device:TPU:0, one launch (start us, length us, event | category | flops | bytes accessed | tf_op | source)
XLA Modules:
  0.0 64.2 jit_solution(14362416574336274390)
XLA Ops:
  0.6 58.8 %shard_map.94 = (bf16[128,1024]{1,0:T(8,128)(2,1)}, bf16[128,128]{1,0:T(8,128)(2,1)}, f32[512,128]{1,0:T(8,128)}) custom-call(bf16[128,8192]{1,0:T(8,128)(2,1)} %cols_ref.1, bf16[128,8192]{1,0:T(8,128)(2,1)} %cols_ref.1, bf16[8192,128]{1,0:T(8,128)(2,1)} %w_ref.1, bf16[128,1024]{1,0:T(8,128)(2,1)} %q_hbm.1, bf16[128,128]{1,0:T(8,128)(2,1)} %k_hbm.1, ...), custom_call_target="tpu_custom_call" | custom-call | tf_op jit(solution)/shard_map/pallas_call | solution.py:301
  59.4 1.7 %copy.13 = bf16[128,1024]{1,0:T(8,128)(2,1)} copy(bf16[128,1024]{1,0:T(8,128)(2,1)} %get-tuple-element.6) | data formatting | bytes 524288
  61.1 1.4 %copy.14 = bf16[128,128]{1,0:T(8,128)(2,1)} copy(bf16[128,128]{1,0:T(8,128)(2,1)} %get-tuple-element.7) | data formatting | bytes 65536
  62.5 1.7 %copy.15 = f32[512,128]{1,0:T(8,128)} copy(f32[512,128]{1,0:T(8,128)} %get-tuple-element.8) | data formatting | bytes 524288

commit v3 on v2

--- a/solution.py
+++ b/solution.py
@@ -32,7 +32,7 @@
 
 
 def kernel(
-    data, ctx, x_ref, cols_ref, w_ref, q_hbm, k_hbm, g_hbm, doc_hbm, route_hbm,
+    data, ctx, tensor, x_ref, cols_ref, w_ref, q_hbm, k_hbm, g_hbm, doc_hbm, route_hbm,
     qg_ref, kg_ref, wg_ref,
     x_buf, w_buf, q_ref, k_ref, g_ref, doc_ref, route_ref, kv_send, kv_recv, q_send, q_recv, kv_all, x_recv,
     red_send, red_recv, dq_send, dq_recv, dkv_send, dkv_recv, vg_all, wg_send, wg_recv,
@@ -52,7 +52,17 @@
     direct = groups == data
     aligned = block % 128 == 0
     ranks = [lax.rem(rank + i, data) for i in range(data)]
-    cols = [lax.rem(col + i, ctx) for i in range(ctx)]
+    shared = aligned and data % 2 == 0 and ctx % 2 == 0 and tensor % 2 == 0
+    if ctx % 2 == 0:
+        core, chip = lax.rem(col, 2), lax.div(col, 2)
+        cores, chips = (core, 1 - core), ctx // 2
+        cols = [2 * lax.rem(chip + i // 2, chips) + cores[i % 2] for i in range(ctx)]
+        sources = [2 * lax.rem(chip + chips - i // 2, chips) + cores[i % 2] for i in range(ctx)]
+    else:
+        cols = [lax.rem(col + i, ctx) for i in range(ctx)]
+    share = lax.axis_index("tensor")
+    half = lax.rem(share, 2)
+    partner = share + 1 - 2 * half
 
     def to_rank(phase, i, src, dst):
         return pltpu.make_async_remote_copy(
@@ -78,6 +88,8 @@
             (route_hbm, route_ref), (doc_hbm, doc_ref), (k_hbm, k_ref), (q_hbm, q_ref), (g_hbm, g_ref)))]
     for copy in small:
         copy.start()
+    if shared:
+        pl.semaphore_signal(barrier, inc=1, device_id={"tensor": partner}, device_id_type=pl.DeviceIdType.MESH)
     loads = []
     for n in range(CHUNKS):
         span = pl.ds(n * step, step)
@@ -87,24 +99,39 @@
         for load in loads[-1]:
             load.start()
 
-    pl.semaphore_wait(barrier, data - 1 + ctx - 1)
-
-    x_out, x_own = [], []
+    pl.semaphore_wait(barrier, data - 1 + ctx - 1 + (1 if shared else 0))
+
+    x_out, x_own, x_direct, x_forward = [], [], [], []
+
+    def columns(d, i):
+        if not aligned:
+            return cols_ref.at[cols[i]]
+        return x_ref.at[:, pl.ds(pl.multiple_of((d * ctx + cols[i]) * block, block), block)]
+
+    def exchange(src, dst, k, i, device):
+        return pltpu.make_async_remote_copy(
+            src_ref=src, dst_ref=dst, send_sem=x_send_sem.at[k, i], recv_sem=x_recv_sem.at[k, i],
+            device_id=device, device_id_type=pl.DeviceIdType.MESH)
+
     for d in range(data if aligned else 1):
-        for i in range(ctx):
-            if aligned:
-                start = pl.multiple_of((d * ctx + cols[i]) * block, block)
-                source = x_ref.at[:, pl.ds(start, block)]
-            else:
-                source = cols_ref.at[cols[i]]
-            if i == 0:
-                x_own.append(pltpu.make_async_copy(source, x_recv.at[d, col], own_sem.at[d]))
-            else:
-                x_out.append(pltpu.make_async_remote_copy(
-                    src_ref=source, dst_ref=x_recv.at[d, col],
-                    send_sem=x_send_sem.at[d, i], recv_sem=x_recv_sem.at[d, i],
-                    device_id={"ctx": cols[i]}, device_id_type=pl.DeviceIdType.MESH))
-    for copy in x_own + x_out:
+        x_own.append(pltpu.make_async_copy(columns(d, 0), x_recv.at[d, col], own_sem.at[d]))
+        for i in range(1, 2 if shared else ctx):
+            x_out.append(exchange(columns(d, i), x_recv.at[d, col], d, i, {"ctx": cols[i]}))
+    if shared:
+        for k in range(data // 2):
+            d = 2 * k + half
+            for i in range(2, ctx):
+                x_direct.append(exchange(columns(d, i), x_recv.at[d, col], k, i, {"ctx": cols[i]}))
+                place = x_recv.at[d, sources[i]]
+                x_forward.append(exchange(place, place, data // 2 + k, i, {"tensor": partner}))
+    middle = len(x_direct) // 2
+
+    def hand_on(first, last):
+        for n in range(first, last):
+            x_direct[n].wait_recv()
+            x_forward[n].start()
+
+    for copy in x_direct + x_own + x_out:
         copy.start()
 
     for copy in small[:3]:
@@ -169,6 +196,7 @@
     queries = arrange(q_recv)
     for copy in gather:
         copy.wait_recv()
+    hand_on(0, middle)
 
     scale = 1.0 / math.sqrt(head)
     pack_len = ctx * seg
@@ -206,6 +234,7 @@
     reduce = [to_col(REDUCE, i, red_send.at[cols[i]], red_recv.at[i]) for i in range(1, ctx)]
     for copy in reduce:
         copy.start()
+    hand_on(middle, len(x_direct))
 
     halves = []
     for p in range(packs):
@@ -249,7 +278,7 @@
     for copy in vgrad:
         copy.start()
     kg_ref[...] = dkv[:, :head]
-    for copy in x_out:
+    for copy in x_out + x_forward:
         copy.wait_recv()
     for copy in x_own:
         copy.wait()
@@ -279,7 +308,7 @@
     for i in range(1, data):
         weight_grad = weight_grad + wg_recv[i].astype(F32)
     wg_ref[...] = weight_grad.T if aligned else weight_grad
-    for copy in kv_out + q_out + x_out + gather + reduce + dq_out + dkv_out + vgrad + wg_out:
+    for copy in kv_out + q_out + x_out + x_direct + x_forward + gather + reduce + dq_out + dkv_out + vgrad + wg_out:
         copy.wait_send()
 
 
@@ -299,7 +328,7 @@
     hbm = pl.BlockSpec(memory_space=pltpu.HBM)
     dma = pltpu.SemaphoreType.DMA
     return pl.pallas_call(
-        functools.partial(kernel, data, ctx),
+        functools.partial(kernel, data, ctx, lax.axis_size("tensor")),
         out_shape=(
             jax.ShapeDtypeStruct((rows, width), BF16),
             jax.ShapeDtypeStruct((rows, head), BF16),

time: 64.4 us -> 53.5 us (0.83)
  Pallas kernels: 58.8 us -> 47.9 us
    pallas_call x1, Pallas kernels: 58.8 us -> 47.9 us  [local(): pl.pallas_call(functools.partial(kernel, data, ctx, lax.axis_size('tensor...]
where the time goes in v3:
time: 53.5 us; the launch traced here: 53.3 us
  Pallas kernels  47.9 us (90%)
  local copies, waits for them, and re-layouts  4.71 us (9%)
  between operations  0.64 us (1%)
    pallas_call x1, Pallas kernels, local(): pl.pallas_call(functools.partial(kernel, data, ctx, lax.axis_size('tensor...  47.9 us
    unnamed x3, local copies, waits for them, and re-layouts  4.71 us

profile of v3, /device:TPU:0, one launch (start us, length us, event | category | flops | bytes accessed | tf_op | source)
XLA Modules:
  0.0 53.3 jit_solution(7817183343509273017)
XLA Ops:
  0.6 47.9 %shard_map.94 = (bf16[128,1024]{1,0:T(8,128)(2,1)}, bf16[128,128]{1,0:T(8,128)(2,1)}, f32[512,128]{1,0:T(8,128)}) custom-call(bf16[128,8192]{1,0:T(8,128)(2,1)} %cols_ref.1, bf16[128,8192]{1,0:T(8,128)(2,1)} %cols_ref.1, bf16[8192,128]{1,0:T(8,128)(2,1)} %w_ref.1, bf16[128,1024]{1,0:T(8,128)(2,1)} %q_hbm.1, bf16[128,128]{1,0:T(8,128)(2,1)} %k_hbm.1, ...), custom_call_target="tpu_custom_call" | custom-call | tf_op jit(solution)/shard_map/pallas_call | solution.py:330
  48.5 1.7 %copy.13 = bf16[128,1024]{1,0:T(8,128)(2,1)} copy(bf16[128,1024]{1,0:T(8,128)(2,1)} %get-tuple-element.6) | data formatting | bytes 524288
  50.2 1.4 %copy.14 = bf16[128,128]{1,0:T(8,128)(2,1)} copy(bf16[128,128]{1,0:T(8,128)(2,1)} %get-tuple-element.7) | data formatting | bytes 65536
  51.6 1.7 %copy.15 = f32[512,128]{1,0:T(8,128)} copy(f32[512,128]{1,0:T(8,128)} %get-tuple-element.8) | data formatting | bytes 524288

commit v4 on v3

--- a/solution.py
+++ b/solution.py
@@ -231,10 +231,11 @@
         red_send[:, p * seg:(p + 1) * seg, head:] = dv.reshape(ctx, seg, head)
         scores_grad.append(ds)
         key_stacks.append(keys)
+        if p == 0:
+            hand_on(middle, len(x_direct))
     reduce = [to_col(REDUCE, i, red_send.at[cols[i]], red_recv.at[i]) for i in range(1, ctx)]
     for copy in reduce:
         copy.start()
-    hand_on(middle, len(x_direct))
 
     halves = []
     for p in range(packs):

time: 53.5 us -> 53.5 us (level)
  no operation moved by 1% of the time
where the time goes in v4:
time: 53.5 us; the launch traced here: 53.3 us
  Pallas kernels  47.9 us (90%)
  local copies, waits for them, and re-layouts  4.71 us (9%)
  between operations  0.64 us (1%)
    pallas_call x1, Pallas kernels, local(): pl.pallas_call(functools.partial(kernel, data, ctx, lax.axis_size('tensor...  47.9 us
    unnamed x3, local copies, waits for them, and re-layouts  4.71 us

profile of v4, /device:TPU:0, one launch (start us, length us, event | category | flops | bytes accessed | tf_op | source)
XLA Modules:
  0.0 53.3 jit_solution(244391902083416347)
XLA Ops:
  0.6 47.9 %shard_map.94 = (bf16[128,1024]{1,0:T(8,128)(2,1)}, bf16[128,128]{1,0:T(8,128)(2,1)}, f32[512,128]{1,0:T(8,128)}) custom-call(bf16[128,8192]{1,0:T(8,128)(2,1)} %cols_ref.1, bf16[128,8192]{1,0:T(8,128)(2,1)} %cols_ref.1, bf16[8192,128]{1,0:T(8,128)(2,1)} %w_ref.1, bf16[128,1024]{1,0:T(8,128)(2,1)} %q_hbm.1, bf16[128,128]{1,0:T(8,128)(2,1)} %k_hbm.1, ...), custom_call_target="tpu_custom_call" | custom-call | tf_op jit(solution)/shard_map/pallas_call | solution.py:331
  48.5 1.7 %copy.13 = bf16[128,1024]{1,0:T(8,128)(2,1)} copy(bf16[128,1024]{1,0:T(8,128)(2,1)} %get-tuple-element.6) | data formatting | bytes 524288
  50.2 1.4 %copy.14 = bf16[128,128]{1,0:T(8,128)(2,1)} copy(bf16[128,128]{1,0:T(8,128)(2,1)} %get-tuple-element.7) | data formatting | bytes 65536
  51.6 1.7 %copy.15 = f32[512,128]{1,0:T(8,128)} copy(f32[512,128]{1,0:T(8,128)} %get-tuple-element.8) | data formatting | bytes 524288
